TPU v7x, 32 devices: a whole 2x2x4 slice. The times are simulated.
32 devices in a mesh: segment: 2 (over core), expert: 16 (over z, y, x).
Axes of the slice: x: 2, y: 2, z: 4, core: 2. Of those that a mesh axis runs over, the one named last changes fastest.
Arguments:
- tokens: bfloat16 [2, 256, 4096], P(None, 'expert'), may hold values from -6 to 6
- expert_ids: int32 [2, 2, 256, 8], P('segment', None, 'expert'), may hold values from 0 to 15, all different within a row; in each aligned block of 16 rows (0 to 15, 16 to 31, ..., all dimensions but the last counted through in order) at most 16 rows name the same one
- gate_weights: float32 [2, 2, 256, 8], P('segment', None, 'expert'), may hold values from 0.05 to 0.5
- norm_gain: float32 [2, 4096], P('segment'), may hold values from 0.25 to 1.75
- w_gate: bfloat16 [2, 16, 4096, 768], P('segment', 'expert'), may hold values from -0.09375 to 0.09375
- w_up: bfloat16 [2, 16, 4096, 768], P('segment', 'expert'), may hold values from -0.09375 to 0.09375
- w_down: bfloat16 [2, 16, 768, 4096], P('segment', 'expert'), may hold values from -0.21875 to 0.21875
Outputs:
- section_out: bfloat16 [2, 2, 256, 4096], P('segment', None, 'expert')
Inputs may be any that keep to these rules, and one draw needn't show every extreme that they name: `expert_ids`: each row names 8 different experts. In each aligned block of 16 rows (the rows of one device for one section and micro-batch) no expert is named more than 16 times, a bound that some block reaches.
All inputs are finite; a program needn't handle non-finite values.
Results may differ from a plain program's by a relative error of at most 0.0059.
Values may be sent and summed in bfloat16 or wider, within the bound.
A program may use at most 128 MiB of HBM per device.

v0:
```python
import jax
import jax.numpy as jnp
from jax import lax
from jax.sharding import PartitionSpec as P


def from_behind(value, axis, steps):
    count = lax.axis_size(axis)
    initial, last = (max(0, -steps), min(count, count - steps))
    return lax.ppermute(value, axis, [(source, source + steps) for source in range(initial, last)])


def norm_rows(current, gain):
    values = current.astype(jnp.float32)
    scaled = values * lax.rsqrt(jnp.mean(values * values, axis=-1, keepdims=True) + 1e-06)
    return (scaled * gain).astype(jnp.bfloat16)


def slot_index(routes, capacity, experts):
    flat = routes.reshape(-1)
    onehot = (flat[:, None] == jnp.arange(experts, dtype=jnp.int32)[None, :]).astype(jnp.int32)
    ranks = jnp.sum(jnp.cumsum(onehot, axis=0) * onehot, axis=1) - 1
    return (flat * capacity + ranks).reshape(routes.shape)


def expert_rows(received, weights):
    gate_all, up_all, down_all = weights
    row_block = received[:, 0].reshape(-1, received.shape[-1])
    gate_part = jnp.dot(row_block, gate_all[0], preferred_element_type=jnp.float32)
    up_part = jnp.dot(row_block, up_all[0], preferred_element_type=jnp.float32)
    hidden = (jax.nn.silu(gate_part) * up_part).astype(jnp.bfloat16)
    result = jnp.dot(hidden, down_all[0], preferred_element_type=jnp.float32).astype(jnp.bfloat16)
    outputs = [result.reshape(received.shape[0], received.shape[2], received.shape[3])]
    return jnp.stack(outputs, axis=1)


def serve_rows(received, weights):
    return lax.all_to_all(
        expert_rows(received, weights), "expert", split_axis=0, concat_axis=0, tiled=True
    )


def pick_rows(gathered, all_routes, member, local, capacity, groups):
    tok_dev = all_routes.shape[0] // groups
    top = all_routes.shape[1]
    blocks = all_routes.reshape(groups, tok_dev * top)
    owners = member * local + jnp.arange(local, dtype=jnp.int32)
    counts = (blocks[:, :, None] == owners[None, None, :]).astype(jnp.int32)
    ranks = jnp.cumsum(counts, axis=1) * counts - 1
    hits = (ranks[..., None] == jnp.arange(capacity, dtype=jnp.int32)).astype(jnp.int32)
    selector = hits.reshape(groups, tok_dev, top, local, capacity).sum(axis=2).astype(jnp.bfloat16)
    features = gathered.reshape(groups, tok_dev, gathered.shape[-1])
    return jnp.einsum(
        "ntec,ntd->necd", selector, features, preferred_element_type=jnp.float32
    ).astype(jnp.bfloat16)


def shards(tokens, expert_ids, gate_weights, norm_gain, w_gate, w_up, w_down):
    micro = tokens.shape[0]
    tok_dev = tokens.shape[1]
    width = tokens.shape[2]
    top = expert_ids.shape[-1]
    groups = lax.axis_size("expert")
    segments = lax.axis_size("segment")
    local = w_gate.shape[1]
    experts = local * groups
    capacity = 2 * tok_dev * top // experts
    segment_no = lax.axis_index("segment")
    member = lax.axis_index("expert")
    gain = norm_gain[0]
    weights = (w_gate[0], w_up[0], w_down[0])
    incoming = jnp.zeros((tok_dev, width), jnp.bfloat16)
    results = jnp.zeros((micro, tok_dev, width), jnp.bfloat16)
    total_ticks = micro + segments - 1
    for tick_no in range(total_ticks):
        offset = tick_no - segment_no
        micro_no = jnp.clip(offset, 0, micro - 1)
        fresh = tokens[min(tick_no, micro - 1)]
        current = jnp.where(segment_no == 0, fresh, incoming)
        routes = lax.dynamic_index_in_dim(expert_ids[0], micro_no, 0, keepdims=False)
        weighting = lax.dynamic_index_in_dim(gate_weights[0], micro_no, 0, keepdims=False)
        normed = norm_rows(current, gain)
        places = slot_index(routes, capacity, experts)
        gathered, all_routes = (
            lax.all_gather(normed, "expert", axis=0, tiled=True),
            lax.all_gather(routes, "expert", axis=0, tiled=True),
        )
        returned = serve_rows(
            pick_rows(gathered, all_routes, member, local, capacity, groups), weights
        )
        flat_back = returned.reshape(-1, width)
        picked = jnp.take(flat_back, places.reshape(-1), axis=0).reshape(tok_dev, top, width)
        mixed = (
            current.astype(jnp.float32)
            + jnp.sum(weighting[:, :, None] * picked.astype(jnp.float32), axis=1)
        ).astype(jnp.bfloat16)
        valid = (offset >= 0) & (offset < micro)
        updated = lax.dynamic_update_index_in_dim(results, mixed, micro_no, 0)
        results = jnp.where(valid, updated, results)
        if tick_no < total_ticks - 1:
            incoming = from_behind(mixed, "segment", 1)
    return results[None]


def solution(mesh):
    in_specs = (
        P(None, "expert", None),
        P("segment", None, "expert", None),
        P("segment", None, "expert", None),
        P("segment", None),
        P("segment", "expert", None, None),
        P("segment", "expert", None, None),
        P("segment", "expert", None, None),
    )
    out_specs = P("segment", None, "expert", None)
    return jax.shard_map(shards, mesh=mesh, in_specs=in_specs, out_specs=out_specs, check_vma=False)
```

profile of v0, /device:TPU:1, one launch (start us, length us, event | category | flops | bytes accessed | tf_op | source)
XLA Modules:
  0.0 452.6 jit_solution(2569357902259863388)
XLA Ops:
  7.6 1.7 fusion.62
  10.7 35.3 %all-gather = s32[1,1,256,8]{3,1,0,2:T(1,128)S(1)} all-gather(s32[1,1,16,8]{3,1,0,2:T(1,128)S(1)} %copy.101), channel_id=2, replica_groups=mesh['segment'=2,'expert'=16] {'expert'}, dimensions={2}, use_global_device_ids=true | all-gather | bytes 8704 | tf_op jit(solution)/shard_map/all_gather | solution.py:86
  47.3 23.3 %fusion.90 = s32[16,128,1,1]{3,0,1,2:T(8,128)S(1)} fusion(s32[16,128,1,1]{3,0,1,2:T(8,128)S(1)} %copy.77), kind=kOutput, calls=%fused_computation.125 | output fusion | flops 260096 | bytes 16384 | tf_op jit(solution)/shard_map/jit(cumsum)/reduce_window_sum | solution.py:49
  70.6 2.2 reduce.5
  73.5 2.3 convolution_convert_fusion.2
  75.9 4.6 %fusion.16 = f32[256,768]{1,0:T(8,128)S(1)} fusion(bf16[256,4096]{1,0:T(8,128)(2,1)S(1)} %bitcast.162, bf16[1,1,4096,768]{3,2,1,0:T(8,128)(2,1)} %param.13), kind=kOutput, calls=%fused_computation.19 | convolution fusion | flops 1610612736 | bytes 9175040 | tf_op jit(solution)/shard_map/dot_general | solution.py:29
  80.4 10.5 %fusion.18 = bf16[256,4096]{1,0:T(8,128)(2,1)} fusion(bf16[1,1,768,4096]{3,2,1,0:T(8,128)(2,1)} %param.15, bf16[256,4096]{1,0:T(8,128)(2,1)S(1)} %bitcast.163, bf16[1,1,4096,768]{3,2,1,0:T(8,128)(2,1)} %param.14, f32[256,768]{1,0:T(8,128)S(1)} %fusion.16), kind=kOutput, calls=%fused_computation.24 | convolution fusion | flops 3223453696 | bytes 17563648 | tf_op jit(solution)/shard_map/dot_general | solution.py:32
  91.0 3.8 all-to-all-start
  96.2 36.7 %all-to-all-done = bf16[16,1,16,4096]{3,2,1,0:T(8,128)(2,1)S(1)} async-done(((bf16[16,1,16,4096]{3,2,1,0:T(8,128)(2,1)}), bf16[16,1,16,4096]{3,2,1,0:T(8,128)(2,1)S(1)}, u32[]{:S(2)}, u32[]{:S(2)}) %all-to-all-start) | async-done | bytes 2097184 | tf_op jit(solution)/shard_map/all_to_all | solution.py:38
  136.9 9.5 %collective-permute-done = bf16[16,4096]{1,0:T(8,128)(2,1)S(1)} collective-permute-done((bf16[16,4096]{1,0:T(8,128)(2,1)S(1)}, bf16[16,4096]{1,0:T(8,128)(2,1)S(1)}, u32[]{:S(2)}, u32[]{:S(2)}) %collective-permute-start) | collective-permute-done | bytes 131104 | tf_op jit(solution)/shard_map/ppermute | solution.py:10
  147.5 35.5 %all-gather.1 = s32[1,1,256,8]{3,1,0,2:T(1,128)S(1)} all-gather(s32[1,1,16,8]{3,1,0,2:T(1,128)S(1)} %copy.102), channel_id=3, replica_groups=mesh['segment'=2,'expert'=16] {'expert'}, dimensions={2}, use_global_device_ids=true | all-gather | bytes 8704 | tf_op jit(solution)/shard_map/all_gather | solution.py:86
  183.0 30.1 %all-gather.2 = s32[1,1,256,8]{3,1,0,2:T(1,128)S(1)} all-gather(s32[1,1,16,8]{3,1,0,2:T(1,128)S(1)} %copy.103), channel_id=4, replica_groups=mesh['segment'=2,'expert'=16] {'expert'}, dimensions={2}, use_global_device_ids=true | all-gather | bytes 8704 | tf_op jit(solution)/shard_map/all_gather | solution.py:86
  213.1 1.7 convert_reduce_fusion.3
  215.7 23.3 %fusion.91 = s32[16,128,1,1]{3,0,1,2:T(8,128)S(1)} fusion(s32[16,128,1,1]{3,0,1,2:T(8,128)S(1)} %copy.85), kind=kOutput, calls=%fused_computation.126 | output fusion | flops 260096 | bytes 16384 | tf_op jit(solution)/shard_map/jit(cumsum)/reduce_window_sum | solution.py:49
  239.0 2.2 reduce.8
  241.9 2.3 convolution_convert_fusion.1
  244.3 4.6 %fusion.14 = f32[256,768]{1,0:T(8,128)S(1)} fusion(bf16[256,4096]{1,0:T(8,128)(2,1)S(1)} %bitcast.164, bf16[1,1,4096,768]{3,2,1,0:T(8,128)(2,1)} %param.13), kind=kOutput, calls=%fused_computation.17 | convolution fusion | flops 1610612736 | bytes 9175040 | tf_op jit(solution)/shard_map/dot_general | solution.py:29
  248.8 10.5 %fusion.21 = bf16[256,4096]{1,0:T(8,128)(2,1)} fusion(bf16[1,1,768,4096]{3,2,1,0:T(8,128)(2,1)} %param.15, bf16[256,4096]{1,0:T(8,128)(2,1)S(1)} %bitcast.165, bf16[1,1,4096,768]{3,2,1,0:T(8,128)(2,1)} %param.14, f32[256,768]{1,0:T(8,128)S(1)} %fusion.14), kind=kOutput, calls=%fused_computation.25 | convolution fusion | flops 3223453696 | bytes 17563648 | tf_op jit(solution)/shard_map/dot_general | solution.py:32
  259.4 3.8 all-to-all-start.1
  267.2 33.1 %all-to-all-done.1 = bf16[16,1,16,4096]{3,2,1,0:T(8,128)(2,1)S(1)} async-done(((bf16[16,1,16,4096]{3,2,1,0:T(8,128)(2,1)}), bf16[16,1,16,4096]{3,2,1,0:T(8,128)(2,1)S(1)}, u32[]{:S(2)}, u32[]{:S(2)}) %all-to-all-start.1) | async-done | bytes 2097184 | tf_op jit(solution)/shard_map/all_to_all | solution.py:38
  303.2 1.6 fusion.79
  306.4 10.5 %collective-permute-done.1 = bf16[16,4096]{1,0:T(8,128)(2,1)S(1)} collective-permute-done((bf16[16,4096]{1,0:T(8,128)(2,1)S(1)}, bf16[16,4096]{1,0:T(8,128)(2,1)S(1)}, u32[]{:S(2)}, u32[]{:S(2)}) %collective-permute-start.1) | collective-permute-done | bytes 131104 | tf_op jit(solution)/shard_map/ppermute | solution.py:10
  318.7 23.3 %fusion.92 = s32[16,128,1,1]{3,0,1,2:T(8,128)S(1)} fusion(s32[16,128,1,1]{3,0,1,2:T(8,128)S(1)} %copy.93), kind=kOutput, calls=%fused_computation.127 | output fusion | flops 260096 | bytes 16384 | tf_op jit(solution)/shard_map/jit(cumsum)/reduce_window_sum | solution.py:49
  342.0 2.2 reduce.11
  344.9 34.4 %all-gather.11.cloned.1.call-done = bf16[256,4096]{1,0:T(8,128)(2,1)} async-done(((bf16[16,4096]{1,0:T(8,128)(2,1)}), bf16[256,4096]{1,0:T(8,128)(2,1)}) %all-gather.11.cloned.1.call-update) | async-done | bytes 2097168 | tf_op jit(solution)/shard_map/all_gather | solution.py:85
  379.3 2.3 convolution_convert_fusion
  381.6 4.6 %fusion.12 = f32[256,768]{1,0:T(8,128)S(1)} fusion(bf16[256,4096]{1,0:T(8,128)(2,1)S(1)} %bitcast.166, bf16[1,1,4096,768]{3,2,1,0:T(8,128)(2,1)} %param.13), kind=kOutput, calls=%fused_computation.15 | convolution fusion | flops 1610612736 | bytes 9175040 | tf_op jit(solution)/shard_map/dot_general | solution.py:29
  386.2 10.5 %fusion.24 = bf16[256,4096]{1,0:T(8,128)(2,1)} fusion(bf16[1,1,768,4096]{3,2,1,0:T(8,128)(2,1)} %param.15, bf16[256,4096]{1,0:T(8,128)(2,1)S(1)} %bitcast.167, bf16[1,1,4096,768]{3,2,1,0:T(8,128)(2,1)} %param.14, f32[256,768]{1,0:T(8,128)S(1)} %fusion.12), kind=kOutput, calls=%fused_computation.26 | convolution fusion | flops 3223453696 | bytes 17563648 | tf_op jit(solution)/shard_map/dot_general | solution.py:32
  396.7 4.0 all-to-all-start.2
  401.5 1.7 copy.109
  403.2 39.2 %all-to-all-done.2 = bf16[16,1,16,4096]{3,2,1,0:T(8,128)(2,1)S(1)} async-done(((bf16[16,1,16,4096]{3,2,1,0:T(8,128)(2,1)}), bf16[16,1,16,4096]{3,2,1,0:T(8,128)(2,1)S(1)}, u32[]{:S(2)}, u32[]{:S(2)}) %all-to-all-start.2) | async-done | bytes 2097184 | tf_op jit(solution)/shard_map/all_to_all | solution.py:38
  444.4 1.6 fusion.76
  (107 shorter events, 25.8 us)
Async XLA Ops:
  6.5 67.0 %all-gather.7.cloned.1.call-start = ((), (), s32[]{:S(2)}) async-start(), calls=%async_computation.3 | async-start | bytes 2228224 | tf_op jit(solution)/shard_map/all_gather | solution.py:85
  91.0 4.1 copy-start.10
  91.0 41.9 %all-to-all-start = ((bf16[16,1,16,4096]{3,2,1,0:T(8,128)(2,1)}), bf16[16,1,16,4096]{3,2,1,0:T(8,128)(2,1)S(1)}, u32[]{:S(2)}, u32[]{:S(2)}) async-start(bf16[16,1,16,4096]{3,2,1,0:T(8,128)(2,1)} %bitcast.160), calls=%async_computation | async-start | bytes 4194304 | tf_op jit(solution)/shard_map/all_to_all | solution.py:38
  94.8 147.1 %all-gather.9.cloned.1.call-start = ((), (), s32[]{:S(2)}) async-start(), calls=%async_computation.4 | async-start | bytes 2228224 | tf_op jit(solution)/shard_map/all_gather | solution.py:85
  132.8 2.8 copy-start
  134.0 12.6 %copy-start.5 = (f32[1,4096]{1,0:T(1,128)S(1)}, f32[1,4096]{1,0:T(1,128)}, u32[]{:S(2)}) copy-start(f32[1,4096]{1,0:T(1,128)} %param.12) | copy-start | bytes 49156
  134.1 13.3 %copy-start.6 = (s32[1,1,16,8]{2,3,1,0:T(8,128)S(1)}, s32[1,1,16,8]{2,3,1,0:T(8,128)}, u32[]{:S(2)}) copy-start(s32[1,1,16,8]{2,3,1,0:T(8,128)} %get-tuple-element.27) | copy-start | bytes 1540
  134.1 13.4 %copy-start.8 = (s32[1,1,16,8]{2,3,1,0:T(8,128)S(1)}, s32[1,1,16,8]{2,3,1,0:T(8,128)}, u32[]{:S(2)}) copy-start(s32[1,1,16,8]{2,3,1,0:T(8,128)} %get-tuple-element.28) | copy-start | bytes 1540
  134.9 0.7 copy-start.1
  135.6 10.8 %collective-permute-start = (bf16[16,4096]{1,0:T(8,128)(2,1)S(1)}, bf16[16,4096]{1,0:T(8,128)(2,1)S(1)}, u32[]{:S(2)}, u32[]{:S(2)}) collective-permute-start(bf16[16,4096]{1,0:T(8,128)(2,1)S(1)} %fusion.63), channel_id=1, source_target_pairs={{0,16},{1,17},{2,18},{3,19},{4,20},{5,21},{6,22},{7,23},{8,24},{9,... | collective-permute-start | bytes 393224 | tf_op jit(solution)/shard_map/ppermute | solution.py:10
  259.3 3.9 copy-start.9
  259.3 4.1 copy-start.12
  259.4 7.1 %copy-start.2 = (f32[16,4096]{1,0:T(8,128)S(1)}, f32[16,4096]{1,0:T(8,128)}, u32[]{:S(2)}) copy-start(f32[16,4096]{1,0:T(8,128)} %copy-done.1) | copy-start | bytes 786436
  259.4 41.0 %all-to-all-start.1 = ((bf16[16,1,16,4096]{3,2,1,0:T(8,128)(2,1)}), bf16[16,1,16,4096]{3,2,1,0:T(8,128)(2,1)S(1)}, u32[]{:S(2)}, u32[]{:S(2)}) async-start(bf16[16,1,16,4096]{3,2,1,0:T(8,128)(2,1)} %bitcast.157), calls=%async_computation.1 | async-start | bytes 4194304 | tf_op jit(solution)/shard_map/all_to_all | solution.py:38
  263.2 116.1 %all-gather.11.cloned.1.call-start = ((), (), s32[]{:S(2)}) async-start(), calls=%async_computation.5 | async-start | bytes 2228224 | tf_op jit(solution)/shard_map/all_gather | solution.py:85
  301.6 16.2 %copy-start.4 = (s32[256,8]{1,0:T(8,128)S(1)}, s32[256,8]{1,0:T(8,128)}, u32[]{:S(2)}) copy-start(s32[256,8]{1,0:T(8,128)} %get-tuple-element.8) | copy-start | bytes 24580
  301.6 16.3 %copy-start.3 = (pred[1,1,256,8]{3,1,0,2:T(4,128)(4,1)S(1)}, pred[1,1,256,8]{3,1,0,2:T(4,128)(4,1)}, u32[]{:S(2)}) copy-start(pred[1,1,256,8]{3,1,0,2:T(4,128)(4,1)} %get-tuple-element.9) | copy-start | bytes 6148
  304.8 12.0 %collective-permute-start.1 = (bf16[16,4096]{1,0:T(8,128)(2,1)S(1)}, bf16[16,4096]{1,0:T(8,128)(2,1)S(1)}, u32[]{:S(2)}, u32[]{:S(2)}) collective-permute-start(bf16[16,4096]{1,0:T(8,128)(2,1)S(1)} %get-tuple-element.13), channel_id=1, source_target_pairs={{0,16},{1,17},{2,18},{3,19},{4,20},{5,21},{6,22},{7,23},{8,24},{9,... | collective-permute-start | bytes 393224 | tf_op jit(solution)/shard_map/ppermute | solution.py:10
  396.7 4.1 copy-start.7
  396.7 4.2 copy-start.11
  396.7 45.7 %all-to-all-start.2 = ((bf16[16,1,16,4096]{3,2,1,0:T(8,128)(2,1)}), bf16[16,1,16,4096]{3,2,1,0:T(8,128)(2,1)S(1)}, u32[]{:S(2)}, u32[]{:S(2)}) async-start(bf16[16,1,16,4096]{3,2,1,0:T(8,128)(2,1)} %bitcast.159), calls=%async_computation.2 | async-start | bytes 4194304 | tf_op jit(solution)/shard_map/all_to_all | solution.py:38
Sparse Core Ops, SparseCore 0:
  10.1 62.6 all-gather.6
  147.5 62.1 all-gather.8
  317.9 61.3 all-gather.10
where the time goes:
time: 460 us; the launch traced here: 453 us
  waiting for transfers between devices  164 us (36%)
  blocking collectives  101 us (22%)
  other arithmetic  94.3 us (20%)
  matrix products  52.3 us (11%)
  starting transfers between devices  14.6 us (3%)
  between operations  13.6 us (3%)
  local copies, waits for them, and re-layouts  13.4 us (3%)
    all_to_all x3, waiting for transfers between devices, serve_rows(): lax.all_to_all(expert_rows(received, weights), 'expert', split_axis=0, co...  109 us
    all_gather x3, blocking collectives, shards(): lax.all_gather(routes, 'expert', axis=0, tiled=True)  101 us
    another operation x6, other arithmetic, pick_rows(): ranks = jnp.cumsum(counts, axis=1) * counts - 1  76.6 us
    all_gather x3, waiting for transfers between devices, shards(): lax.all_gather(normed, 'expert', axis=0, tiled=True)  34.5 us
    dot_general x3, matrix products, expert_rows(): jnp.dot(hidden, down_all[0], preferred_element_type=jnp.float32)  31.5 us
    ppermute x2, waiting for transfers between devices, from_behind(): lax.ppermute(value, axis, [(source, source + steps) for source in range(i...  20 us
    dot_general x3, matrix products, expert_rows(): jnp.dot(row_block, gate_all[0], preferred_element_type=jnp.float32)  13.7 us
    all_to_all x3, starting transfers between devices, serve_rows(): lax.all_to_all(expert_rows(received, weights), 'expert', split_axis=0, co...  11.7 us
  transfers between devices with their start and end apart: 8, of which 6 were waited for; matrix products, arithmetic and copies ran while one was open for 20% of the time, Pallas kernels for 0%

commit v1 on v0

--- a/solution.py
+++ b/solution.py
@@ -1,7 +1,397 @@
+import functools
+
 import jax
 import jax.numpy as jnp
 from jax import lax
+from jax.experimental import pallas as pl
+from jax.experimental.pallas import tpu as pltpu
 from jax.sharding import PartitionSpec as P
+
+PLANE = 4
+CHUNKS = 4
+LANES = 128
+VMEM_BYTES = 60 * 1024 * 1024
+MESH = pl.DeviceIdType.MESH
+
+
+def vmem_need(micro, tok_dev, width, ff, groups):
+    rows = tok_dev * groups
+    weights = 3 * width * ff * 2
+    features = 2 * micro * rows * width * 2
+    landing = micro * (rows // PLANE) * width * 2 * 4 + micro * tok_dev * width * 2 * 6
+    hidden = rows * ff * (8 + 2) + rows * LANES * 4
+    return weights + features + landing + hidden
+
+
+def relay_kernel(
+    micro, segments, groups, tok_dev, width, ff, chunks,
+    tok, ids, gw, gain, wg, wu, wd, out,
+    xg, cur, outb, part, r1, r2, r3, zb, gb, wgv, wuv, wdv, acc, hid,
+    wsem, zs, zr, xs, xr, fs, fr, r1s, r1r, r2s, r2r, r3s, r3r, cs, cr,
+):
+    depth = groups // PLANE
+    wide = width // chunks
+    bundle = depth * tok_dev
+    half = bundle // 2
+    seg = lax.axis_index("segment")
+    me = lax.axis_index("expert")
+    yx = me % PLANE
+    z = me // PLANE
+    xn = yx + 1 - 2 * (yx % 2)
+    yn = yx + 2 - 4 * (yx // 2)
+    across = PLANE - 1 - yx
+    x_dev = z * PLANE + xn
+    y_dev = z * PLANE + yn
+
+    def rows(start, size):
+        return pl.ds(pl.multiple_of(start, 16), size)
+
+    def peer(d):
+        return (z + d) % depth
+
+    own_rows = rows((yx * depth + z) * tok_dev, tok_dev)
+
+    def bundle_rows(which):
+        return rows(which * bundle, bundle)
+
+    def first_rows(which):
+        return rows(which * bundle, half)
+
+    def last_rows(which):
+        return rows(which * bundle + half, half)
+
+    def send(src, dst, s, r, dev):
+        return pltpu.make_async_remote_copy(
+            src_ref=src, dst_ref=dst, send_sem=s, recv_sem=r, device_id=(seg, dev), device_id_type=MESH
+        )
+
+    def feature(m, c):
+        return gb if c is None else xg.at[m, c]
+
+    def slot(c):
+        return chunks if c is None else c
+
+    def z_copy(m, c, d):
+        ref = feature(m, c).at[own_rows]
+        return send(ref, ref, zs.at[m, slot(c), d - 1], zr.at[m, slot(c), d - 1], peer(d) * PLANE + yx)
+
+    def xy_copy(m, c, a):
+        ref = feature(m, c).at[bundle_rows(yx)]
+        return send(ref, ref, xs.at[m, slot(c), a], xr.at[m, slot(c), a], (x_dev, y_dev)[a])
+
+    def f_copy(m, c, a):
+        ref = feature(m, c).at[(first_rows(xn), last_rows(yn))[a]]
+        return send(ref, ref, fs.at[m, slot(c), a], fr.at[m, slot(c), a], (y_dev, x_dev)[a])
+
+    def z_send(m, c):
+        for d in range(1, depth):
+            z_copy(m, c, d).start()
+
+    def xy_send(m, c):
+        for d in range(1, depth):
+            z_copy(m, c, d).wait_recv()
+        for a in range(2):
+            xy_copy(m, c, a).start()
+
+    def f_send(m, c):
+        for a in range(2):
+            xy_copy(m, c, a).wait_recv()
+            f_copy(m, c, a).start()
+
+    def f_wait(m, c):
+        for a in range(2):
+            f_copy(m, c, a).wait_recv()
+
+    def r1_copy(m, c, a):
+        ref = part.at[m, c, (first_rows(across), last_rows(across))[a]]
+        return send(ref, r1.at[m, c, a], r1s.at[m, c, a], r1r.at[m, c, a], (y_dev, x_dev)[a])
+
+    def r2_copy(m, c, a):
+        ref = part.at[m, c, bundle_rows((xn, yn)[a])]
+        return send(ref, r2.at[m, c, a], r2s.at[m, c, a], r2r.at[m, c, a], (x_dev, y_dev)[a])
+
+    def r3_copy(m, c, d):
+        ref = zb.at[m, c, rows(peer(d) * tok_dev, tok_dev)]
+        return send(ref, r3.at[m, c, d - 1], r3s.at[m, c, d - 1], r3r.at[m, c, d - 1], peer(d) * PLANE + yx)
+
+    def relay_copy(m, c):
+        return pltpu.make_async_remote_copy(
+            src_ref=outb.at[m, c], dst_ref=cur.at[m, c], send_sem=cs.at[m, c], recv_sem=cr.at[m, c],
+            device_id=(1 - seg, me), device_id_type=MESH,
+        )
+
+    f32 = jnp.float32
+
+    def r2_send(m, c):
+        for a in range(2):
+            r1_copy(m, c, a).wait_recv()
+            into = (first_rows(xn), last_rows(yn))[a]
+            part[m, c, into] = (part[m, c, into].astype(f32) + r1[m, c, a].astype(f32)).astype(jnp.bfloat16)
+            r2_copy(m, c, a).start()
+
+    def r3_send(m, c):
+        for a in range(2):
+            r2_copy(m, c, a).wait_recv()
+        total = part[m, c, bundle_rows(yx)].astype(f32) + r2[m, c, 0].astype(f32) + r2[m, c, 1].astype(f32)
+        zb[m, c] = total.astype(jnp.bfloat16)
+        for d in range(1, depth):
+            r3_copy(m, c, d).start()
+
+    def finish(m, c):
+        for d in range(1, depth):
+            r3_copy(m, c, d).wait_recv()
+        inside = rows(z * tok_dev, tok_dev)
+        total = part[m, c, own_rows].astype(f32) + r2[m, c, 0, inside].astype(f32) + r2[m, c, 1, inside].astype(f32)
+        for d in range(1, depth):
+            total = total + r3[m, c, d - 1].astype(f32)
+        value = (cur[m, c].astype(f32) + total).astype(jnp.bfloat16)
+        outb[m, c] = value
+        out[m, :, pl.ds(pl.multiple_of(c * wide, LANES), wide)] = value
+
+        @pl.when(seg == 0)
+        def _():
+            relay_copy(m, c).start()
+
+    def weight_copy(which, c):
+        src = (
+            wg.at[rows(c * wide, wide)], wu.at[rows(c * wide, wide)],
+            wd.at[:, pl.ds(pl.multiple_of(c * wide, LANES), wide)],
+        )[which]
+        return pltpu.make_async_copy(src, (wgv, wuv, wdv)[which].at[c], wsem.at[which, c])
+
+    def up_chunk(m, c):
+        f_wait(m, c)
+
+        @pl.when(m == 0)
+        def _():
+            weight_copy(0, c).wait()
+            weight_copy(1, c).wait()
+
+        x = xg[m, c]
+        gate = jnp.dot(x, wgv[c], preferred_element_type=f32)
+        up = jnp.dot(x, wuv[c], preferred_element_type=f32)
+
+        @pl.when(c == 0)
+        def _():
+            acc[0] = gate
+            acc[1] = up
+
+        @pl.when(c > 0)
+        def _():
+            acc[0] += gate
+            acc[1] += up
+
+    experts = groups
+
+    def down_chunk(m, c):
+        @pl.when(m == 0)
+        def _():
+            weight_copy(2, c).wait()
+
+        lane = lax.broadcasted_iota(jnp.int32, (groups * tok_dev, LANES), 1)
+        gate = jnp.sum(jnp.where(lane == m * experts + me, gb[...], 0.0), axis=1, keepdims=True)
+        value = jnp.dot(hid[...], wdv[c], preferred_element_type=f32)
+        part[m, c] = (value * gate).astype(jnp.bfloat16)
+        for a in range(2):
+            r1_copy(m, c, a).start()
+
+    def take_in(m):
+        @pl.when(seg == 0)
+        def _():
+            for c in range(chunks):
+                cur[m, c] = tok[m, :, c * wide:(c + 1) * wide]
+
+        @pl.when(seg > 0)
+        def _():
+            for c in range(chunks):
+                relay_copy(m, c).wait_recv()
+
+        square = jnp.zeros((tok_dev, 1), f32)
+        for c in range(chunks):
+            value = cur[m, c].astype(f32)
+            square = square + jnp.sum(value * value, axis=1, keepdims=True)
+        scale = lax.rsqrt(square / width + 1e-6)
+        for c in range(chunks):
+            value = cur[m, c].astype(f32) * scale * gain[:, c * wide:(c + 1) * wide]
+            xg[m, c, own_rows] = value.astype(jnp.bfloat16)
+            z_send(m, c)
+
+    barrier = pltpu.get_barrier_semaphore()
+    partners = [(seg, peer(d) * PLANE + yx) for d in range(1, depth)]
+    partners += [(seg, x_dev), (seg, y_dev), (1 - seg, me)]
+    for partner in partners:
+        pl.semaphore_signal(barrier, inc=1, device_id=partner, device_id_type=MESH)
+    for c in range(chunks):
+        weight_copy(0, c).start()
+        weight_copy(1, c).start()
+    for c in range(chunks):
+        weight_copy(2, c).start()
+
+    lane = lax.broadcasted_iota(jnp.int32, (tok_dev, LANES), 1)
+    gates = jnp.zeros((tok_dev, LANES), f32)
+    for m in range(micro):
+        for k in range(ids.shape[-1]):
+            hit = lane == ids[m, :, k:k + 1] + m * experts
+            gates = gates + jnp.where(hit, gw[m, :, k:k + 1], 0.0)
+    gb[own_rows] = gates
+    pl.semaphore_wait(barrier, len(partners))
+
+    def stage(m, carry):
+        @pl.when(m < micro)
+        def _():
+            take_in(m)
+
+        @pl.when(m == 0)
+        def _():
+            z_send(0, None)
+
+        def step(t, carry):
+            new = m < micro
+            old = m > 0
+
+            @pl.when(new & (t < chunks))
+            def _():
+                xy_send(m, t)
+
+            @pl.when((m == 0) & (t == 0))
+            def _():
+                xy_send(0, None)
+
+            @pl.when(old & (t < chunks))
+            def _():
+                down_chunk(m - 1, t)
+
+            @pl.when(new & (t >= 1) & (t < chunks + 1))
+            def _():
+                f_send(m, t - 1)
+
+            @pl.when((m == 0) & (t == 1))
+            def _():
+                f_send(0, None)
+
+            @pl.when(old & (t >= 1) & (t < chunks + 1))
+            def _():
+                r2_send(m - 1, t - 1)
+
+            @pl.when(old & (t >= 2) & (t < chunks + 2))
+            def _():
+                r3_send(m - 1, t - 2)
+
+            @pl.when(new & (t >= 2) & (t < chunks + 2))
+            def _():
+                up_chunk(m, t - 2)
+
+            @pl.when((m == 0) & (t == 2))
+            def _():
+                f_wait(0, None)
+
+            @pl.when(old & (t >= 3))
+            def _():
+                finish(m - 1, t - 3)
+
+            return carry
+
+        lax.fori_loop(0, chunks + 3, step, 0)
+
+        @pl.when(m < micro)
+        def _():
+            gate = acc[0]
+            hid[...] = (gate * jax.nn.sigmoid(gate) * acc[1]).astype(jnp.bfloat16)
+
+        return carry
+
+    lax.fori_loop(0, micro + 1, stage, 0)
+
+    def sent(m, c, with_return):
+        for d in range(1, depth):
+            z_copy(m, c, d).wait_send()
+        for a in range(2):
+            xy_copy(m, c, a).wait_send()
+            f_copy(m, c, a).wait_send()
+        if with_return:
+            for a in range(2):
+                r1_copy(m, c, a).wait_send()
+                r2_copy(m, c, a).wait_send()
+            for d in range(1, depth):
+                r3_copy(m, c, d).wait_send()
+
+            @pl.when(seg == 0)
+            def _():
+                relay_copy(m, c).wait_send()
+
+    def drain(i, carry):
+        sent(i // chunks, i % chunks, True)
+        return carry
+
+    lax.fori_loop(0, micro * chunks, drain, 0)
+    sent(0, None, False)
+
+
+def fused(tokens, expert_ids, gate_weights, norm_gain, w_gate, w_up, w_down):
+    micro, tok_dev, width = tokens.shape
+    ff = w_gate.shape[-1]
+    groups = lax.axis_size("expert")
+    segments = lax.axis_size("segment")
+    depth = groups // PLANE
+    rows = groups * tok_dev
+    bundle = depth * tok_dev
+    chunks = CHUNKS
+    wide = width // chunks
+    bf16 = jnp.bfloat16
+    dma = pltpu.SemaphoreType.DMA
+    vmem = pl.BlockSpec(memory_space=pltpu.VMEM)
+    hbm = pl.BlockSpec(memory_space=pl.ANY)
+    scratch = [
+        pltpu.VMEM((micro, chunks, rows, wide), bf16),
+        pltpu.VMEM((micro, chunks, tok_dev, wide), bf16),
+        pltpu.VMEM((micro, chunks, tok_dev, wide), bf16),
+        pltpu.VMEM((micro, chunks, rows, wide), bf16),
+        pltpu.VMEM((micro, chunks, 2, bundle // 2, wide), bf16),
+        pltpu.VMEM((micro, chunks, 2, bundle, wide), bf16),
+        pltpu.VMEM((micro, chunks, depth - 1, tok_dev, wide), bf16),
+        pltpu.VMEM((micro, chunks, bundle, wide), bf16),
+        pltpu.VMEM((rows, LANES), jnp.float32),
+        pltpu.VMEM((chunks, wide, ff), bf16),
+        pltpu.VMEM((chunks, wide, ff), bf16),
+        pltpu.VMEM((chunks, ff, wide), bf16),
+        pltpu.VMEM((2, rows, ff), jnp.float32),
+        pltpu.VMEM((rows, ff), bf16),
+        dma((3, chunks)),
+    ]
+    for count, kinds in ((chunks + 1, (depth - 1, 2, 2)), (chunks, (2, 2, depth - 1))):
+        for kind in kinds:
+            scratch += [dma((micro, count, kind))] * 2
+    scratch += [dma((micro, chunks))] * 2
+    result = pl.pallas_call(
+        functools.partial(relay_kernel, micro, segments, groups, tok_dev, width, ff, chunks),
+        out_shape=jax.ShapeDtypeStruct((micro, tok_dev, width), bf16),
+        in_specs=[vmem, vmem, vmem, vmem, hbm, hbm, hbm],
+        out_specs=vmem,
+        scratch_shapes=scratch,
+        compiler_params=pltpu.CompilerParams(
+            collective_id=0, has_side_effects=True, vmem_limit_bytes=VMEM_BYTES
+        ),
+        cost_estimate=pl.CostEstimate(
+            flops=micro * 6 * rows * width * ff, bytes_accessed=3 * width * ff * 2, transcendentals=micro * rows * ff
+        ),
+    )(tokens, expert_ids[0], gate_weights[0], norm_gain, w_gate[0, 0], w_up[0, 0], w_down[0, 0])
+    return result[None]
+
+
+def fits(tokens, expert_ids, w_gate):
+    micro, tok_dev, width = tokens.shape
+    groups = lax.axis_size("expert")
+    return (
+        lax.axis_size("segment") == 2
+        and w_gate.shape[1] == 1
+        and groups % PLANE == 0
+        and groups > PLANE
+        and (groups // PLANE) % 2 == 0
+        and tok_dev % 16 == 0
+        and width % (CHUNKS * LANES) == 0
+        and micro * groups <= LANES
+        and vmem_need(micro, tok_dev, width, w_gate.shape[3], groups) < VMEM_BYTES * 4 // 5
+    )
 
 
 def from_behind(value, axis, steps):
@@ -56,6 +446,8 @@
 
 
 def shards(tokens, expert_ids, gate_weights, norm_gain, w_gate, w_up, w_down):
+    if fits(tokens, expert_ids, w_gate):
+        return fused(tokens, expert_ids, gate_weights, norm_gain, w_gate, w_up, w_down)
     micro = tokens.shape[0]
     tok_dev = tokens.shape[1]
     width = tokens.shape[2]

time: 460 us -> 132 us (0.29); the launches traced: 453 us -> 132 us
  waiting for transfers between devices: 164 us -> 0 us
  Pallas kernels: 0 us -> 128 us
  blocking collectives: 101 us -> 0 us
  other arithmetic: 94.3 us -> 0 us
  matrix products: 52.3 us -> 0 us
  starting transfers between devices: 14.6 us -> 0 us
  between operations: 13.6 us -> 0.01 us
  local copies, waits for them, and re-layouts: 13.4 us -> 4.41 us
    pallas_call x0 -> x1, Pallas kernels: none -> 128 us  [fused(): pl.pallas_call(functools.partial(relay_kernel, micro, segments, groups, t...]
    all_to_all x3 -> x0, waiting for transfers between devices: 109 us -> none  [serve_rows(): lax.all_to_all(expert_rows(received, weights), 'expert', split_axis=0, co...]
    all_gather x3 -> x0, blocking collectives: 101 us -> none  [shards(): lax.all_gather(routes, 'expert', axis=0, tiled=True)]
    another operation x9 -> x0, other arithmetic: 77.1 us -> none  [the longest x6 76.6 us: pick_rows(): ranks = jnp.cumsum(counts, axis=1) * counts - 1]
    dot_general x9 -> x0, matrix products: 52.3 us -> none  [the longest x3 31.5 us: expert_rows(): jnp.dot(hidden, down_all[0], preferred_element_type=jnp.float32)]
    all_gather x3 -> x0, waiting for transfers between devices: 34.5 us -> none  [shards(): lax.all_gather(normed, 'expert', axis=0, tiled=True)]
    ppermute x2 -> x0, waiting for transfers between devices: 20 us -> none  [from_behind(): lax.ppermute(value, axis, [(source, source + steps) for source in range(i...]
    all_to_all x3 -> x0, starting transfers between devices: 11.7 us -> none  [serve_rows(): lax.all_to_all(expert_rows(received, weights), 'expert', split_axis=0, co...]
  transfers between devices with their start and end apart: 8 -> 0, of which waited for: 6 -> 0; matrix products, arithmetic and copies ran while one was open for 20% -> 0% of each run, Pallas kernels for 0% -> 0%
where the time goes in v1:
time: 132 us
  Pallas kernels  128 us (97%)
  local copies, waits for them, and re-layouts  4.41 us (3%)
    pallas_call x1, Pallas kernels, fused(): pl.pallas_call(functools.partial(relay_kernel, micro, segments, groups, t...  128 us
    unnamed x3, local copies, waits for them, and re-layouts  4.41 us

profile of v1, /device:TPU:1, one launch (start us, length us, event | category | flops | bytes accessed | tf_op | source)
XLA Modules:
  0.0 132.2 jit_solution(8877905186325694817)
XLA Ops:
  0.0 1.4 %copy.8 = s32[1,2,16,8]{3,2,1,0:T(8,128)} copy(s32[1,2,16,8]{2,3,1,0:T(8,128)} %param.8) | data formatting | bytes 2048 | tf_op args[1]
  1.4 1.4 %copy.9 = f32[1,2,16,8]{3,2,1,0:T(8,128)} copy(f32[1,2,16,8]{2,3,1,0:T(8,128)} %param.9) | data formatting | bytes 2048 | tf_op args[2]
  2.7 127.8 %shard_map.73 = bf16[2,16,4096]{2,1,0:T(8,128)(2,1)} custom-call(bf16[2,16,4096]{2,1,0:T(8,128)(2,1)} %tok.1, s32[2,16,8]{2,1,0:T(8,128)} %bitcast.7, f32[2,16,8]{2,1,0:T(8,128)} %bitcast.8, f32[1,4096]{1,0:T(1,128)} %gain.1, bf16[4096,768]{1,0:T(8,128)(2,1)} %bitcast.9, bf16[4096,768]{1,0:T(8,128)(2,1)} %bitcast.10, bf16[768,4096]{1,0:T(8,128)(2,1)} %bitcast.11), custom_call_target="tpu_custom_call" | custom-call | flops 9663676416 | bytes 18874368 | tf_op jit(solution)/shard_map/pallas_call | solution.py:365
  130.5 1.7 %copy.11 = bf16[1,2,16,4096]{3,2,1,0:T(8,128)(2,1)} copy(bf16[1,2,16,4096]{3,2,1,0:T(8,128)(2,1)} %bitcast.6) | data formatting | bytes 524288

commit v2 on v1

--- a/solution.py
+++ b/solution.py
@@ -216,6 +216,10 @@
             xg[m, c, own_rows] = value.astype(jnp.bfloat16)
             z_send(m, c)
 
+    def hidden():
+        gate = acc[0]
+        hid[...] = (gate * jax.nn.sigmoid(gate) * acc[1]).astype(jnp.bfloat16)
+
     barrier = pltpu.get_barrier_semaphore()
     partners = [(seg, peer(d) * PLANE + yx) for d in range(1, depth)]
     partners += [(seg, x_dev), (seg, y_dev), (1 - seg, me)]
@@ -227,80 +231,56 @@
     for c in range(chunks):
         weight_copy(2, c).start()
 
-    lane = lax.broadcasted_iota(jnp.int32, (tok_dev, LANES), 1)
-    gates = jnp.zeros((tok_dev, LANES), f32)
+    row = lax.broadcasted_iota(jnp.int32, (LANES, tok_dev), 0)
+    gates = jnp.zeros((LANES, tok_dev), f32)
     for m in range(micro):
-        for k in range(ids.shape[-1]):
-            hit = lane == ids[m, :, k:k + 1] + m * experts
-            gates = gates + jnp.where(hit, gw[m, :, k:k + 1], 0.0)
-    gb[own_rows] = gates
+        for k in range(ids.shape[1]):
+            hit = row == ids[m, k:k + 1] + m * experts
+            gates = gates + jnp.where(hit, gw[m, k:k + 1], 0.0)
+    gb[own_rows] = gates.T
     pl.semaphore_wait(barrier, len(partners))
 
-    def stage(m, carry):
-        @pl.when(m < micro)
-        def _():
-            take_in(m)
-
-        @pl.when(m == 0)
-        def _():
-            z_send(0, None)
-
-        def step(t, carry):
-            new = m < micro
-            old = m > 0
-
-            @pl.when(new & (t < chunks))
-            def _():
-                xy_send(m, t)
-
-            @pl.when((m == 0) & (t == 0))
-            def _():
-                xy_send(0, None)
-
-            @pl.when(old & (t < chunks))
-            def _():
-                down_chunk(m - 1, t)
-
-            @pl.when(new & (t >= 1) & (t < chunks + 1))
-            def _():
-                f_send(m, t - 1)
-
-            @pl.when((m == 0) & (t == 1))
-            def _():
-                f_send(0, None)
-
-            @pl.when(old & (t >= 1) & (t < chunks + 1))
-            def _():
-                r2_send(m - 1, t - 1)
-
-            @pl.when(old & (t >= 2) & (t < chunks + 2))
-            def _():
-                r3_send(m - 1, t - 2)
-
-            @pl.when(new & (t >= 2) & (t < chunks + 2))
-            def _():
-                up_chunk(m, t - 2)
-
-            @pl.when((m == 0) & (t == 2))
-            def _():
-                f_wait(0, None)
-
-            @pl.when(old & (t >= 3))
-            def _():
-                finish(m - 1, t - 3)
-
-            return carry
-
-        lax.fori_loop(0, chunks + 3, step, 0)
-
-        @pl.when(m < micro)
-        def _():
-            gate = acc[0]
-            hid[...] = (gate * jax.nn.sigmoid(gate) * acc[1]).astype(jnp.bfloat16)
+    take_in(0)
+    z_send(0, None)
+
+    late = 5 * seg
+    plan = (
+        (r3_send, 0, 12), (r3_send, 1, 19 + late), (r2_send, 0, 10), (r2_send, 1, 17 + late),
+        (xy_send, 0, 0), (xy_send, 1, 5 + late), (f_send, 0, 2), (f_send, 1, 7 + late),
+        (finish, 0, 14), (finish, 1, 21 + late), (up_chunk, 0, 4), (up_chunk, 1, 11 + late),
+        (down_chunk, 0, 8), (down_chunk, 1, 15 + late),
+    )
+
+    def step(s, carry):
+        @pl.when(s == 5 + late)
+        def _():
+            take_in(1)
+
+        @pl.when(s == 4)
+        def _():
+            xy_send(0, None)
+
+        @pl.when(s == 6)
+        def _():
+            f_send(0, None)
+
+        @pl.when(s == 8)
+        def _():
+            f_wait(0, None)
+            hidden()
+
+        @pl.when(s == 15 + late)
+        def _():
+            hidden()
+
+        for action, m, first in plan:
+            @pl.when((s >= first) & (s < first + chunks))
+            def _(action=action, m=m, first=first):
+                action(m, s - first)
 
         return carry
 
-    lax.fori_loop(0, micro + 1, stage, 0)
+    lax.fori_loop(0, 21 + chunks + late, step, 0)
 
     def sent(m, c, with_return):
         for d in range(1, depth):
@@ -374,7 +354,7 @@
         cost_estimate=pl.CostEstimate(
             flops=micro * 6 * rows * width * ff, bytes_accessed=3 * width * ff * 2, transcendentals=micro * rows * ff
         ),
-    )(tokens, expert_ids[0], gate_weights[0], norm_gain, w_gate[0, 0], w_up[0, 0], w_down[0, 0])
+    )(tokens, jnp.swapaxes(expert_ids[0], 1, 2), jnp.swapaxes(gate_weights[0], 1, 2), norm_gain, w_gate[0, 0], w_up[0, 0], w_down[0, 0])
     return result[None]
 
 

time: 132 us -> 117 us (0.89)
  Pallas kernels: 128 us -> 115 us
  local copies, waits for them, and re-layouts: 4.41 us -> 1.67 us
    pallas_call x1, Pallas kernels: 128 us -> 115 us  [fused(): pl.pallas_call(functools.partial(relay_kernel, micro, segments, groups, t...]
    unnamed x3 -> x1, local copies, waits for them, and re-layouts: 4.41 us -> 1.67 us
where the time goes in v2:
time: 117 us
  Pallas kernels  115 us (98%)
  local copies, waits for them, and re-layouts  1.67 us (1%)
    pallas_call x1, Pallas kernels, fused(): pl.pallas_call(functools.partial(relay_kernel, micro, segments, groups, t...  115 us

profile of v2, /device:TPU:1, one launch (start us, length us, event | category | flops | bytes accessed | tf_op | source)
XLA Modules:
  0.0 117.1 jit_solution(1851575339787301037)
XLA Ops:
  0.0 115.4 %shard_map.73 = bf16[2,16,4096]{2,1,0:T(8,128)(2,1)} custom-call(bf16[2,16,4096]{2,1,0:T(8,128)(2,1)} %tok.1, s32[2,8,16]{2,1,0:T(8,128)} %bitcast.14, f32[2,8,16]{2,1,0:T(8,128)} %bitcast.15, f32[1,4096]{1,0:T(1,128)} %gain.1, bf16[4096,768]{1,0:T(8,128)(2,1)} %bitcast.11, bf16[4096,768]{1,0:T(8,128)(2,1)} %bitcast.12, bf16[768,4096]{1,0:T(8,128)(2,1)} %bitcast.13), custom_call_target="tpu_custom_call" | custom-call | flops 9663676416 | bytes 18874368 | tf_op jit(solution)/shard_map/pallas_call | solution.py:345
  115.4 1.7 %copy.9 = bf16[1,2,16,4096]{3,2,1,0:T(8,128)(2,1)} copy(bf16[1,2,16,4096]{3,2,1,0:T(8,128)(2,1)} %bitcast.10) | data formatting | bytes 524288

commit v3 on v2

--- a/solution.py
+++ b/solution.py
@@ -243,33 +243,44 @@
     take_in(0)
     z_send(0, None)
 
-    late = 5 * seg
+    def at(first, relayed):
+        return first + (relayed - first) * seg
+
+    n = chunks
+    take_at = at(n - 2, 2 * n + 9)
+    gates_at = n
+    down_0 = n + 4
+    down_1 = at(3 * n + 4, 3 * n + 14)
+    fin_1 = at(3 * n + 12, 3 * n + 20)
     plan = (
-        (r3_send, 0, 12), (r3_send, 1, 19 + late), (r2_send, 0, 10), (r2_send, 1, 17 + late),
-        (xy_send, 0, 0), (xy_send, 1, 5 + late), (f_send, 0, 2), (f_send, 1, 7 + late),
-        (finish, 0, 14), (finish, 1, 21 + late), (up_chunk, 0, 4), (up_chunk, 1, 11 + late),
-        (down_chunk, 0, 8), (down_chunk, 1, 15 + late),
+        (r3_send, 0, n + 9), (r3_send, 1, at(3 * n + 9, 3 * n + 18)),
+        (r2_send, 0, n + 6), (r2_send, 1, at(3 * n + 6, 3 * n + 16)),
+        (xy_send, 0, 0), (xy_send, 1, at(n + 2, 2 * n + 10)),
+        (f_send, 0, 2), (f_send, 1, at(n + 5, 2 * n + 12)),
+        (finish, 0, n + 12), (finish, 1, fin_1),
+        (up_chunk, 0, 4), (up_chunk, 1, at(2 * n + 4, 2 * n + 14)),
+        (down_chunk, 0, down_0), (down_chunk, 1, down_1),
     )
 
     def step(s, carry):
-        @pl.when(s == 5 + late)
+        @pl.when(s == take_at)
         def _():
             take_in(1)
 
-        @pl.when(s == 4)
+        @pl.when(s == gates_at)
         def _():
             xy_send(0, None)
 
-        @pl.when(s == 6)
+        @pl.when(s == gates_at + 2)
         def _():
             f_send(0, None)
 
-        @pl.when(s == 8)
+        @pl.when(s == down_0)
         def _():
             f_wait(0, None)
             hidden()
 
-        @pl.when(s == 15 + late)
+        @pl.when(s == down_1)
         def _():
             hidden()
 
@@ -280,7 +291,7 @@
 
         return carry
 
-    lax.fori_loop(0, 21 + chunks + late, step, 0)
+    lax.fori_loop(0, fin_1 + n, step, 0)
 
     def sent(m, c, with_return):
         for d in range(1, depth):

time: 117 us -> 119 us (1.017)
  Pallas kernels: 115 us -> 117 us
    pallas_call x1, Pallas kernels: 115 us -> 117 us  [fused(): pl.pallas_call(functools.partial(relay_kernel, micro, segments, groups, t...]
where the time goes in v3:
time: 119 us
  Pallas kernels  117 us (98%)
  local copies, waits for them, and re-layouts  1.67 us (1%)
    pallas_call x1, Pallas kernels, fused(): pl.pallas_call(functools.partial(relay_kernel, micro, segments, groups, t...  117 us

profile of v3, /device:TPU:1, one launch (start us, length us, event | category | flops | bytes accessed | tf_op | source)
XLA Modules:
  0.0 119.0 jit_solution(1382302000568941770)
XLA Ops:
  0.0 117.3 %shard_map.73 = bf16[2,16,4096]{2,1,0:T(8,128)(2,1)} custom-call(bf16[2,16,4096]{2,1,0:T(8,128)(2,1)} %tok.1, s32[2,8,16]{2,1,0:T(8,128)} %bitcast.14, f32[2,8,16]{2,1,0:T(8,128)} %bitcast.15, f32[1,4096]{1,0:T(1,128)} %gain.1, bf16[4096,768]{1,0:T(8,128)(2,1)} %bitcast.11, bf16[4096,768]{1,0:T(8,128)(2,1)} %bitcast.12, bf16[768,4096]{1,0:T(8,128)(2,1)} %bitcast.13), custom_call_target="tpu_custom_call" | custom-call | flops 9663676416 | bytes 18874368 | tf_op jit(solution)/shard_map/pallas_call | solution.py:356
  117.3 1.7 %copy.9 = bf16[1,2,16,4096]{3,2,1,0:T(8,128)(2,1)} copy(bf16[1,2,16,4096]{3,2,1,0:T(8,128)(2,1)} %bitcast.10) | data formatting | bytes 524288

commit v4 on v3

--- a/solution.py
+++ b/solution.py
@@ -137,7 +137,18 @@
         for d in range(1, depth):
             r3_copy(m, c, d).start()
 
+    def gather_sent(m, c):
+        for d in range(1, depth):
+            z_copy(m, c, d).wait_send()
+        for a in range(2):
+            xy_copy(m, c, a).wait_send()
+            f_copy(m, c, a).wait_send()
+
     def finish(m, c):
+        gather_sent(m, c)
+        for a in range(2):
+            r1_copy(m, c, a).wait_send()
+            r2_copy(m, c, a).wait_send()
         for d in range(1, depth):
             r3_copy(m, c, d).wait_recv()
         inside = rows(z * tok_dev, tok_dev)
@@ -247,18 +258,18 @@
         return first + (relayed - first) * seg
 
     n = chunks
-    take_at = at(n - 2, 2 * n + 9)
+    take_at = at(n - 2, n + 8)
     gates_at = n
     down_0 = n + 4
-    down_1 = at(3 * n + 4, 3 * n + 14)
-    fin_1 = at(3 * n + 12, 3 * n + 20)
+    down_1 = at(3 * n + 4, 2 * n + 14)
+    fin_1 = at(3 * n + 12, 2 * n + 20)
     plan = (
-        (r3_send, 0, n + 9), (r3_send, 1, at(3 * n + 9, 3 * n + 18)),
-        (r2_send, 0, n + 6), (r2_send, 1, at(3 * n + 6, 3 * n + 16)),
-        (xy_send, 0, 0), (xy_send, 1, at(n + 2, 2 * n + 10)),
-        (f_send, 0, 2), (f_send, 1, at(n + 5, 2 * n + 12)),
+        (r3_send, 0, n + 9), (r3_send, 1, at(3 * n + 9, 2 * n + 18)),
+        (r2_send, 0, n + 6), (r2_send, 1, at(3 * n + 6, 2 * n + 16)),
+        (xy_send, 0, 0), (xy_send, 1, at(n + 2, n + 10)),
+        (f_send, 0, 2), (f_send, 1, at(n + 5, n + 12)),
         (finish, 0, n + 12), (finish, 1, fin_1),
-        (up_chunk, 0, 4), (up_chunk, 1, at(2 * n + 4, 2 * n + 14)),
+        (up_chunk, 0, 4), (up_chunk, 1, at(2 * n + 4, n + 14)),
         (down_chunk, 0, down_0), (down_chunk, 1, down_1),
     )
 
@@ -293,29 +304,20 @@
 
     lax.fori_loop(0, fin_1 + n, step, 0)
 
-    def sent(m, c, with_return):
-        for d in range(1, depth):
-            z_copy(m, c, d).wait_send()
-        for a in range(2):
-            xy_copy(m, c, a).wait_send()
-            f_copy(m, c, a).wait_send()
-        if with_return:
-            for a in range(2):
-                r1_copy(m, c, a).wait_send()
-                r2_copy(m, c, a).wait_send()
-            for d in range(1, depth):
-                r3_copy(m, c, d).wait_send()
-
-            @pl.when(seg == 0)
-            def _():
-                relay_copy(m, c).wait_send()
-
     def drain(i, carry):
-        sent(i // chunks, i % chunks, True)
+        m = i // chunks
+        c = i % chunks
+        for d in range(1, depth):
+            r3_copy(m, c, d).wait_send()
+
+        @pl.when(seg == 0)
+        def _():
+            relay_copy(m, c).wait_send()
+
         return carry
 
     lax.fori_loop(0, micro * chunks, drain, 0)
-    sent(0, None, False)
+    gather_sent(0, None)
 
 
 def fused(tokens, expert_ids, gate_weights, norm_gain, w_gate, w_up, w_down):

time: 119 us -> 112 us (0.941)
  Pallas kernels: 117 us -> 110 us
    pallas_call x1, Pallas kernels: 117 us -> 110 us  [fused(): pl.pallas_call(functools.partial(relay_kernel, micro, segments, groups, t...]
where the time goes in v4:
time: 112 us
  Pallas kernels  110 us (98%)
  local copies, waits for them, and re-layouts  1.67 us (1%)
    pallas_call x1, Pallas kernels, fused(): pl.pallas_call(functools.partial(relay_kernel, micro, segments, groups, t...  110 us

profile of v4, /device:TPU:1, one launch (start us, length us, event | category | flops | bytes accessed | tf_op | source)
XLA Modules:
  0.0 111.7 jit_solution(6544905637294470444)
XLA Ops:
  0.0 110.0 %shard_map.73 = bf16[2,16,4096]{2,1,0:T(8,128)(2,1)} custom-call(bf16[2,16,4096]{2,1,0:T(8,128)(2,1)} %tok.1, s32[2,8,16]{2,1,0:T(8,128)} %bitcast.14, f32[2,8,16]{2,1,0:T(8,128)} %bitcast.15, f32[1,4096]{1,0:T(1,128)} %gain.1, bf16[4096,768]{1,0:T(8,128)(2,1)} %bitcast.11, bf16[4096,768]{1,0:T(8,128)(2,1)} %bitcast.12, bf16[768,4096]{1,0:T(8,128)(2,1)} %bitcast.13), custom_call_target="tpu_custom_call" | custom-call | flops 9663676416 | bytes 18874368 | tf_op jit(solution)/shard_map/pallas_call | solution.py:358
  110.0 1.7 %copy.9 = bf16[1,2,16,4096]{3,2,1,0:T(8,128)(2,1)} copy(bf16[1,2,16,4096]{3,2,1,0:T(8,128)(2,1)} %bitcast.10) | data formatting | bytes 524288

commit v5 on v4

--- a/solution.py
+++ b/solution.py
@@ -8,7 +8,7 @@
 from jax.sharding import PartitionSpec as P
 
 PLANE = 4
-CHUNKS = 4
+CHUNKS = 8
 LANES = 128
 VMEM_BYTES = 60 * 1024 * 1024
 MESH = pl.DeviceIdType.MESH

time: 112 us -> 127 us (1.13)
  Pallas kernels: 110 us -> 126 us
    pallas_call x1, Pallas kernels: 110 us -> 126 us  [fused(): pl.pallas_call(functools.partial(relay_kernel, micro, segments, groups, t...]
where the time goes in v5:
time: 127 us
  Pallas kernels  126 us (99%)
  local copies, waits for them, and re-layouts  1.67 us (1%)
    pallas_call x1, Pallas kernels, fused(): pl.pallas_call(functools.partial(relay_kernel, micro, segments, groups, t...  126 us

profile of v5, /device:TPU:1, one launch (start us, length us, event | category | flops | bytes accessed | tf_op | source)
XLA Modules:
  0.0 127.3 jit_solution(16928700413335567624)
XLA Ops:
  0.0 125.6 %shard_map.73 = bf16[2,16,4096]{2,1,0:T(8,128)(2,1)} custom-call(bf16[2,16,4096]{2,1,0:T(8,128)(2,1)} %tok.1, s32[2,8,16]{2,1,0:T(8,128)} %bitcast.14, f32[2,8,16]{2,1,0:T(8,128)} %bitcast.15, f32[1,4096]{1,0:T(1,128)} %gain.1, bf16[4096,768]{1,0:T(8,128)(2,1)} %bitcast.11, bf16[4096,768]{1,0:T(8,128)(2,1)} %bitcast.12, bf16[768,4096]{1,0:T(8,128)(2,1)} %bitcast.13), custom_call_target="tpu_custom_call" | custom-call | flops 9663676416 | bytes 18874368 | tf_op jit(solution)/shard_map/pallas_call | solution.py:358
  125.6 1.7 %copy.9 = bf16[1,2,16,4096]{3,2,1,0:T(8,128)(2,1)} copy(bf16[1,2,16,4096]{3,2,1,0:T(8,128)(2,1)} %bitcast.10) | data formatting | bytes 524288

commit v6 on v5

--- a/solution.py
+++ b/solution.py
@@ -8,7 +8,7 @@
 from jax.sharding import PartitionSpec as P
 
 PLANE = 4
-CHUNKS = 8
+CHUNKS = 2
 LANES = 128
 VMEM_BYTES = 60 * 1024 * 1024
 MESH = pl.DeviceIdType.MESH
@@ -258,17 +258,17 @@
         return first + (relayed - first) * seg
 
     n = chunks
-    take_at = at(n - 2, n + 8)
+    take_at = at(n - 1, n + 8)
     gates_at = n
     down_0 = n + 4
     down_1 = at(3 * n + 4, 2 * n + 14)
-    fin_1 = at(3 * n + 12, 2 * n + 20)
+    fin_1 = at(3 * n + 10, 2 * n + 20)
     plan = (
-        (r3_send, 0, n + 9), (r3_send, 1, at(3 * n + 9, 2 * n + 18)),
+        (r3_send, 0, n + 8), (r3_send, 1, at(3 * n + 8, 2 * n + 18)),
         (r2_send, 0, n + 6), (r2_send, 1, at(3 * n + 6, 2 * n + 16)),
         (xy_send, 0, 0), (xy_send, 1, at(n + 2, n + 10)),
         (f_send, 0, 2), (f_send, 1, at(n + 5, n + 12)),
-        (finish, 0, n + 12), (finish, 1, fin_1),
+        (finish, 0, n + 10), (finish, 1, fin_1),
         (up_chunk, 0, 4), (up_chunk, 1, at(2 * n + 4, n + 14)),
         (down_chunk, 0, down_0), (down_chunk, 1, down_1),
     )

time: 127 us -> 119 us (0.937)
  Pallas kernels: 126 us -> 117 us
    pallas_call x1, Pallas kernels: 126 us -> 117 us  [fused(): pl.pallas_call(functools.partial(relay_kernel, micro, segments, groups, t...]
where the time goes in v6:
time: 119 us; the launch traced here: 118 us
  Pallas kernels  117 us (98%)
  local copies, waits for them, and re-layouts  1.67 us (1%)
    pallas_call x1, Pallas kernels, fused(): pl.pallas_call(functools.partial(relay_kernel, micro, segments, groups, t...  117 us

profile of v6, /device:TPU:1, one launch (start us, length us, event | category | flops | bytes accessed | tf_op | source)
XLA Modules:
  0.0 118.4 jit_solution(17946919013658383115)
XLA Ops:
  0.0 116.7 %shard_map.73 = bf16[2,16,4096]{2,1,0:T(8,128)(2,1)} custom-call(bf16[2,16,4096]{2,1,0:T(8,128)(2,1)} %tok.1, s32[2,8,16]{2,1,0:T(8,128)} %bitcast.14, f32[2,8,16]{2,1,0:T(8,128)} %bitcast.15, f32[1,4096]{1,0:T(1,128)} %gain.1, bf16[4096,768]{1,0:T(8,128)(2,1)} %bitcast.11, bf16[4096,768]{1,0:T(8,128)(2,1)} %bitcast.12, bf16[768,4096]{1,0:T(8,128)(2,1)} %bitcast.13), custom_call_target="tpu_custom_call" | custom-call | flops 9663676416 | bytes 18874368 | tf_op jit(solution)/shard_map/pallas_call | solution.py:358
  116.7 1.7 %copy.9 = bf16[1,2,16,4096]{3,2,1,0:T(8,128)(2,1)} copy(bf16[1,2,16,4096]{3,2,1,0:T(8,128)(2,1)} %bitcast.10) | data formatting | bytes 524288

commit v7 on v6

--- a/solution.py
+++ b/solution.py
@@ -8,7 +8,7 @@
 from jax.sharding import PartitionSpec as P
 
 PLANE = 4
-CHUNKS = 2
+CHUNKS = 4
 LANES = 128
 VMEM_BYTES = 60 * 1024 * 1024
 MESH = pl.DeviceIdType.MESH
@@ -258,7 +258,7 @@
         return first + (relayed - first) * seg
 
     n = chunks
-    take_at = at(n - 1, n + 8)
+    take_at = at(n - 2, n + 8)
     gates_at = n
     down_0 = n + 4
     down_1 = at(3 * n + 4, 2 * n + 14)

time: 119 us -> 116 us (0.975)
  Pallas kernels: 117 us -> 114 us
    pallas_call x1, Pallas kernels: 117 us -> 114 us  [fused(): pl.pallas_call(functools.partial(relay_kernel, micro, segments, groups, t...]
where the time goes in v7:
time: 116 us; the launch traced here: 115 us
  Pallas kernels  114 us (98%)
  local copies, waits for them, and re-layouts  1.67 us (1%)
    pallas_call x1, Pallas kernels, fused(): pl.pallas_call(functools.partial(relay_kernel, micro, segments, groups, t...  114 us

profile of v7, /device:TPU:1, one launch (start us, length us, event | category | flops | bytes accessed | tf_op | source)
XLA Modules:
  0.0 115.4 jit_solution(4602423591365190952)
XLA Ops:
  0.0 113.7 %shard_map.73 = bf16[2,16,4096]{2,1,0:T(8,128)(2,1)} custom-call(bf16[2,16,4096]{2,1,0:T(8,128)(2,1)} %tok.1, s32[2,8,16]{2,1,0:T(8,128)} %bitcast.14, f32[2,8,16]{2,1,0:T(8,128)} %bitcast.15, f32[1,4096]{1,0:T(1,128)} %gain.1, bf16[4096,768]{1,0:T(8,128)(2,1)} %bitcast.11, bf16[4096,768]{1,0:T(8,128)(2,1)} %bitcast.12, bf16[768,4096]{1,0:T(8,128)(2,1)} %bitcast.13), custom_call_target="tpu_custom_call" | custom-call | flops 9663676416 | bytes 18874368 | tf_op jit(solution)/shard_map/pallas_call | solution.py:358
  113.7 1.7 %copy.9 = bf16[1,2,16,4096]{3,2,1,0:T(8,128)(2,1)} copy(bf16[1,2,16,4096]{3,2,1,0:T(8,128)(2,1)} %bitcast.10) | data formatting | bytes 524288
